TPU v7x, 32 devices: a whole 2x2x4 slice. The times are simulated.
32 devices in a mesh: parts: 2 (over y), row: 4 (over z), col: 4 (over x, core).
Axes of the slice: x: 2, y: 2, z: 4, core: 2. Of those that a mesh axis runs over, the one named last changes fastest.
Arguments:
- features: bfloat16 [16384, 256], P(('parts', 'row', 'col')), parts along dimension 0, may hold values from -6 to 6
- weight: bfloat16 [256, 256], replicated, may hold values from -0.375 to 0.375
- bias: float32 [256], replicated, may hold values from -3 to 3
- tiles: bfloat16 [8, 4, 256, 128, 128], P(('parts', 'row'), 'col'), parts along dimension 0, may hold values from -0.0625 to 0.0625
- tile_out: int32 [8, 4, 256], P(('parts', 'row'), 'col'), parts along dimension 0, may hold values from 0 to 15
- tile_in: int32 [8, 4, 256], P(('parts', 'row'), 'col'), parts along dimension 0, may hold values from 0 to 15
- tile_count: int32 [8, 4], P(('parts', 'row'), 'col'), parts along dimension 0, may hold values from 64 to 256, as said below
- cotangent: bfloat16 [16384, 256], P(('parts', 'row', 'col')), parts along dimension 0, may hold values from -6 to 6
Outputs:
- output: bfloat16 [16384, 256], P(('parts', 'row', 'col')), parts along dimension 0
- grad_features: bfloat16 [16384, 256], P(('parts', 'row', 'col')), parts along dimension 0
- grad_weight: float32 [512, 256], P('parts'), parts along dimension 0
- grad_bias: float32 [512], P('parts'), parts along dimension 0
There are 2 independent parts, one for each index of `parts`. A program takes and returns all parts, laid end to end along the dimension named above; an argument that names none is the same for every part. Nothing has to cross between parts.
Inputs may be any that keep to these rules, and one draw needn't show every extreme that they name: The live slots of a cell are its first tile_count slots; at least one cell has all 256 slots live.
All inputs are finite; a program needn't handle non-finite values.
Results may differ from a plain program's by a relative error of at most 0.006.
Values may be sent and summed in bfloat16 or wider, within the bound.
A program may use at most 128 MiB of HBM per device.

v0:
```python
import math

import jax
import jax.numpy as jnp
from jax import lax
from jax.sharding import PartitionSpec as P


def accumulate(cell_tiles, from_ids, into_ids, live_count, source, into_count, pattern):
    slot_count = cell_tiles.shape[0]
    from_count = source.shape[0]
    cluster_size = source.shape[1]
    feat_width = source.shape[2]
    span_size = 32
    flat_source = source.reshape(from_count, cluster_size * feat_width)
    initial = jnp.zeros((into_count, cluster_size * feat_width), jnp.float32)
    from_range = jnp.arange(from_count, dtype=jnp.int32)
    into_range = jnp.arange(into_count, dtype=jnp.int32)

    def one_block(block_index, running):
        offset = block_index * span_size
        some_tiles = lax.dynamic_slice_in_dim(cell_tiles, offset, span_size, 0)
        from_block = lax.dynamic_slice_in_dim(from_ids, offset, span_size, 0)
        into_block = lax.dynamic_slice_in_dim(into_ids, offset, span_size, 0)
        is_live = offset + jnp.arange(span_size, dtype=jnp.int32) < live_count
        select = (from_block[:, None] == from_range[None, :]).astype(jnp.bfloat16)
        picked = jnp.dot(select, flat_source, preferred_element_type=jnp.float32).astype(
            jnp.bfloat16
        )
        picked = picked.reshape(span_size, cluster_size, feat_width)
        products = jnp.einsum(pattern, some_tiles, picked, preferred_element_type=jnp.float32)
        placing = ((into_range[:, None] == into_block[None, :]) & is_live[None, :]).astype(
            jnp.float32
        )
        added = jnp.dot(
            placing,
            products.reshape(span_size, cluster_size * feat_width),
            precision=lax.Precision.HIGHEST,
            preferred_element_type=jnp.float32,
        )
        return running + added

    block_total = (live_count + span_size - 1) // span_size
    result = lax.fori_loop(0, block_total, one_block, initial)
    return result.reshape(into_count, cluster_size, feat_width)


def slope(hidden, cotangent):
    gate_value = jax.nn.sigmoid(hidden)
    return (
        cotangent.astype(jnp.float32) * gate_value * (1.0 + hidden * (1.0 - gate_value))
    ).astype(jnp.bfloat16)


def body(features, weight, bias, tiles, tile_out, tile_in, tile_count, cotangent):
    slot_count = tiles.shape[2]
    cluster_size = tiles.shape[3]
    feat_width = features.shape[1]
    own_rows = features.shape[0]
    own_clusters = own_rows // cluster_size
    cell_tiles = tiles.reshape(slot_count, cluster_size, cluster_size)
    out_local = tile_out.reshape(slot_count)
    in_local = tile_in.reshape(slot_count)
    live_count = tile_count.reshape(())
    row_devices = lax.axis_size("row")
    col_devices = lax.axis_size("col")
    into_clusters = own_clusters * row_devices
    from_clusters = own_clusters * col_devices
    projected = jnp.dot(features, weight, preferred_element_type=jnp.float32).astype(jnp.bfloat16)
    inputs = lax.all_gather(projected, "col", axis=0, tiled=True)
    partials = accumulate(
        cell_tiles,
        in_local,
        out_local,
        live_count,
        inputs.reshape(from_clusters, cluster_size, feat_width),
        into_clusters,
        "tij,tjd->tid",
    )
    partials = partials.reshape(into_clusters * cluster_size, feat_width)
    summed = lax.psum_scatter(partials, "row", scatter_dimension=0, tiled=True)
    hidden = summed + bias
    output = jax.nn.silu(hidden).astype(jnp.bfloat16)
    own_grad = slope(hidden, cotangent)
    targets = lax.all_gather(own_grad, "row", axis=0, tiled=True)
    grad_partials = accumulate(
        cell_tiles,
        out_local,
        in_local,
        live_count,
        targets.reshape(into_clusters, cluster_size, feat_width),
        from_clusters,
        "tji,tjd->tid",
    )
    grad_partials = grad_partials.reshape(from_clusters * cluster_size, feat_width)
    grad_proj = lax.psum_scatter(grad_partials, "col", scatter_dimension=0, tiled=True).astype(
        jnp.bfloat16
    )
    grad_features = jnp.dot(grad_proj, weight.T, preferred_element_type=jnp.float32).astype(
        jnp.bfloat16
    )
    local_weight = jnp.dot(features.T, grad_proj, preferred_element_type=jnp.float32)
    local_bias = jnp.sum(own_grad.astype(jnp.float32), axis=0)
    grad_weight, grad_bias = lax.psum((local_weight, local_bias), ("row", "col"))
    factor = 1.0 / math.sqrt(own_rows * row_devices * col_devices)
    return (output, grad_features, grad_weight * factor, grad_bias * factor)


def solution(mesh):
    placed = (
        P(("parts", "row", "col"), None),
        P(),
        P(),
        P(("parts", "row"), "col", None, None, None),
        P(("parts", "row"), "col", None),
        P(("parts", "row"), "col", None),
        P(("parts", "row"), "col"),
        P(("parts", "row", "col"), None),
    )
    return jax.shard_map(
        body,
        mesh=mesh,
        in_specs=placed,
        out_specs=(
            P(("parts", "row", "col"), None),
            P(("parts", "row", "col"), None),
            P("parts", None),
            P("parts"),
        ),
        check_vma=False,
    )
```

profile of v0, /device:TPU:0, one launch (start us, length us, event | category | flops | bytes accessed | tf_op | source)
XLA Modules:
  0.0 389.0 jit_solution(13898876547902860460)
XLA Ops:
  7.2 0.9 copy-done
  8.1 1.8 convolution_convert_fusion.3
  10.7 18.9 %all-gather.3.cloned.1.call-done = bf16[2048,256]{1,0:T(8,128)(2,1)} async-done(((bf16[512,256]{1,0:T(8,128)(2,1)}), bf16[2048,256]{1,0:T(8,128)(2,1)}) %all-gather.3.cloned.1.call-update) | async-done | bytes 1048592 | tf_op jit(solution)/shard_map/all_gather | solution.py:70
  29.6 1.6 reshape_reshape.12
  31.3 27.6 %while.26 = (s32[]{:T(128)}, f32[16,32768]{1,0:T(8,128)S(1)}, s32[]{:T(128)}, s32[256]{0:T(256)S(1)}, s32[]{:T(128)}, /*index=5*/bf16[256,128,128]{2,1,0:T(8,128...) while((s32[]{:T(128)}, f32[16,32768]{1,0:T(8,128)S(1)}, ...), condition=%wide.region_1.2_spmd.clone.clone, body=%wide.region_0.1_spmd.clone.clone.sunk | while | flops 504890944 | bytes 31458296 | solution.py:44
  31.4 0.7 add_compare_fusion.4
  32.2 0.7 convolution_convert_fusion.6
  33.4 1.9 fusion.49
  35.3 2.4 copy.25
  37.8 2.7 convolution_add_fusion.4
  40.5 0.7 add_compare_fusion.4
  41.3 0.7 convolution_convert_fusion.6
  42.6 1.9 fusion.49
  44.5 2.4 copy.25
  47.0 2.7 convolution_add_fusion.4
  49.7 0.7 add_compare_fusion.4
  50.5 0.7 convolution_convert_fusion.6
  51.8 1.9 fusion.49
  53.7 2.4 copy.25
  56.1 2.7 convolution_add_fusion.4
  58.9 1.5 reshape_reshape.13
  60.5 89.8 %reduce-scatter.3.cloned.1.call-done = f32[512,256]{1,0:T(8,128)} async-done(((f32[2048,256]{1,0:T(8,128)}), f32[512,256]{1,0:T(8,128)}) %reduce-scatter.3.cloned.1.call-update) | async-done | bytes 524304 | tf_op jit(solution)/shard_map/reduce_scatter | solution.py:81
  150.3 2.1 convert_reduce_fusion
  152.4 12.0 %copy.12 = bf16[1,1,256,128,128]{3,4,2,1,0:T(8,128)(2,1)} copy(bf16[1,1,256,128,128]{4,3,2,1,0:T(8,128)(2,1)} %bitcast.63) | data formatting | bytes 16777216 | tf_op args[3]
  164.4 15.4 %all-gather.5.cloned.1.call-done = bf16[2048,256]{1,0:T(8,128)(2,1)} async-done(((bf16[512,256]{1,0:T(8,128)(2,1)}), bf16[2048,256]{1,0:T(8,128)(2,1)}) %all-gather.5.cloned.1.call-update) | async-done | bytes 1048592 | tf_op jit(solution)/shard_map/all_gather | solution.py:85
  179.8 1.6 reshape_reshape.14
  181.5 27.7 %while.27 = (s32[]{:T(128)}, f32[16,32768]{1,0:T(8,128)S(1)}, s32[]{:T(128)}, s32[256]{0:T(256)S(1)}, s32[]{:T(128)}, /*index=5*/bf16[256,128,128]{1,2,0:T(8,128...) while((s32[]{:T(128)}, f32[16,32768]{1,0:T(8,128)S(1)}, ...), condition=%wide.region_4.5_spmd.clone.clone, body=%wide.region_3.4_spmd.clone.clone.sunk | while | flops 504890944 | bytes 31458296 | solution.py:44
  181.7 0.7 add_compare_fusion.5
  182.5 0.7 convolution_convert_fusion.7
  183.7 1.9 fusion.55
  185.7 2.4 copy.27
  188.1 2.7 convolution_add_fusion.5
  191.7 0.7 convolution_convert_fusion.7
  192.9 1.9 fusion.55
  194.9 2.4 copy.27
  197.3 2.7 convolution_add_fusion.5
  200.9 0.7 convolution_convert_fusion.7
  202.1 1.9 fusion.55
  204.0 2.4 copy.27
  206.5 2.7 convolution_add_fusion.5
  209.2 1.5 reshape_reshape.15
  210.8 73.7 %psum.15 = f32[256]{0:T(256)S(1)} all-reduce(f32[256]{0:T(256)S(1)} %get-tuple-element.286), channel_id=1, replica_groups=mesh['parts'=2,'row'=4,'col'=4] {'row','col'}, use_global_device_ids=true, to_apply=%region_8.9 | all-reduce | flops 256 | bytes 2048 | tf_op jit(solution)/shard_map/psum | solution.py:104
  285.1 2.9 reduce-scatter.5.cloned.1.call-done
  288.0 2.0 convolution_bitcast_fusion
  290.0 2.0 convolution_convert_fusion.2
  292.0 88.6 %all-reduce.2.cloned.1.call-done = f32[256,256]{0,1:T(8,128)} async-done(((f32[256,256]{0,1:T(8,128)}), f32[256,256]{0,1:T(8,128)}) %all-reduce.2.cloned.1.call-update) | async-done | bytes 262160 | tf_op jit(solution)/shard_map/psum | solution.py:104
  380.7 1.0 broadcast_multiply_fusion
  381.6 0.8 copy.14
  (44 shorter events, 6.3 us)
Async XLA Ops:
  7.2 1.0 copy-start
  7.2 22.4 %all-gather.3.cloned.1.call-start = ((), (), s32[]{:S(2)}) async-start(), calls=%async_computation.2 | async-start | bytes 1310720 | tf_op jit(solution)/shard_map/all_gather | solution.py:70
  10.0 140.3 %reduce-scatter.3.cloned.1.call-start = ((), (), s32[]{:S(2)}) async-start(), calls=%async_computation.3 | async-start | bytes 2621440 | tf_op jit(solution)/shard_map/reduce_scatter | solution.py:81
  10.7 20.6 %copy-start.4 = (s32[1,1,256]{2,1,0:T(1,128)S(1)}, s32[1,1,256]{2,1,0:T(1,128)}, u32[]{:S(2)}) copy-start(s32[1,1,256]{2,1,0:T(1,128)} %param.16) | copy-start | bytes 3076
  10.7 20.6 %copy-start.5 = (s32[1,1,256]{2,1,0:T(1,128)S(1)}, s32[1,1,256]{2,1,0:T(1,128)}, u32[]{:S(2)}) copy-start(s32[1,1,256]{2,1,0:T(1,128)} %param.17) | copy-start | bytes 3076
  60.4 89.8 %copy-start.2 = (bf16[512,256]{1,0:T(8,128)(2,1)S(1)}, bf16[512,256]{1,0:T(8,128)(2,1)}, u32[]{:S(2)}) copy-start(bf16[512,256]{1,0:T(8,128)(2,1)} %param.19) | copy-start | bytes 786436
  60.4 89.8 %copy-start.3 = (f32[256]{0:T(256)S(1)}, f32[256]{0:T(256)}, u32[]{:S(2)}) copy-start(f32[256]{0:T(256)} %param.14) | copy-start | bytes 3076
  60.4 119.3 %all-gather.5.cloned.1.call-start = ((), (), s32[]{:S(2)}) async-start(), calls=%async_computation.4 | async-start | bytes 1310720 | tf_op jit(solution)/shard_map/all_gather | solution.py:85
  152.4 135.6 %reduce-scatter.5.cloned.1.call-start = ((), (), s32[]{:S(2)}) async-start(), calls=%async_computation.5 | async-start | bytes 2621440 | tf_op jit(solution)/shard_map/reduce_scatter | solution.py:96
  210.7 79.3 %copy-start.1 = (bf16[256,256]{1,0:T(8,128)(2,1)S(1)}, bf16[256,256]{1,0:T(8,128)(2,1)}, u32[]{:S(2)}) copy-start(bf16[256,256]{1,0:T(8,128)(2,1)} %param.13) | copy-start | bytes 393220
  210.8 169.9 %all-reduce.2.cloned.1.call-start = ((), (), s32[]{:S(2)}) async-start(), calls=%async_computation.6 | async-start | bytes 524288 | tf_op jit(solution)/shard_map/psum | solution.py:104
Sparse Core Ops, SparseCore 0:
  10.1 19.4 all-gather.2
  60.6 89.6 reduce-scatter.2
  152.5 27.2 all-gather.4
  210.9 77.0 reduce-scatter.4
  291.8 88.8 all-reduce.1
where the time goes:
time: 390 us; the launch traced here: 389 us
  waiting for transfers between devices  216 us (55%)
  blocking collectives  73.7 us (19%)
  local copies, waits for them, and re-layouts  38.6 us (10%)
  matrix products  38.2 us (10%)
  between operations  14.5 us (4%)
  other arithmetic  7.55 us (2%)
    reduce_scatter x1, waiting for transfers between devices, body(): summed = lax.psum_scatter(partials, 'row', scatter_dimension=0, tiled=True)  89.8 us
    psum x1, waiting for transfers between devices, body(): lax.psum((local_weight, local_bias), ('row', 'col'))  88.6 us
    psum x1, blocking collectives, body(): lax.psum((local_weight, local_bias), ('row', 'col'))  73.7 us
    all_gather x1, waiting for transfers between devices, body(): inputs = lax.all_gather(projected, 'col', axis=0, tiled=True)  18.9 us
    while x12, local copies, waits for them, and re-layouts  17.5 us
    dot_general x6, matrix products, one_block(): jnp.dot(placing, products.reshape(span_size, cluster_size * feat_width),...  16.4 us
    all_gather x1, waiting for transfers between devices, body(): targets = lax.all_gather(own_grad, 'row', axis=0, tiled=True)  15.4 us
    unnamed x14, local copies, waits for them, and re-layouts  13.8 us
  transfers between devices with their start and end apart: 5, of which 5 were waited for; matrix products, arithmetic and copies ran while one was open for 4% of the time, Pallas kernels for 0%

commit v1 on v0

--- a/solution.py
+++ b/solution.py
@@ -1,9 +1,14 @@
+import functools
 import math
 
 import jax
 import jax.numpy as jnp
 from jax import lax
+from jax.experimental import pallas as pl
+from jax.experimental.pallas import tpu as pltpu
 from jax.sharding import PartitionSpec as P
+
+MESH = pl.DeviceIdType.MESH
 
 
 def accumulate(cell_tiles, from_ids, into_ids, live_count, source, into_count, pattern):
@@ -105,6 +110,284 @@
     factor = 1.0 / math.sqrt(own_rows * row_devices * col_devices)
     return (output, grad_features, grad_weight * factor, grad_bias * factor)
 
+def build_kernel(count_ref, out_ids, in_ids, tiles_ref, dense_ref, sums):
+    step = pl.program_id(0)
+    slots, size = tiles_ref.shape[0], tiles_ref.shape[1]
+    side = dense_ref.shape[0] // size
+    wide = dense_ref.shape[1] // size
+    spare = side * wide
+
+    @pl.when(step == 0)
+    def _():
+        sums[...] = jnp.zeros_like(sums)
+
+    def add(slot, _):
+        where = step * slots + slot
+        pair = out_ids[where] * wide + in_ids[where]
+        pair = jnp.where(where < count_ref[0], pair, spare)
+        sums[pair] += tiles_ref[slot].astype(jnp.float32)
+        return 0
+
+    lax.fori_loop(0, slots, add, 0, unroll=8)
+
+    @pl.when(step == pl.num_programs(0) - 1)
+    def _():
+        def write(o, _):
+            rows = pl.ds(pl.multiple_of(o * size, size), size)
+            for i in range(wide):
+                dense_ref[rows, pl.ds(i * size, size)] = sums[o * wide + i].astype(jnp.bfloat16)
+            return 0
+
+        lax.fori_loop(0, side, write, 0)
+
+
+def build_dense(cell_tiles, out_local, in_local, live_count, side, wide):
+    slot_count, size, _ = cell_tiles.shape
+    span = 32
+    return pl.pallas_call(
+        build_kernel,
+        out_shape=jax.ShapeDtypeStruct((side * size, wide * size), jnp.bfloat16),
+        grid_spec=pltpu.PrefetchScalarGridSpec(
+            num_scalar_prefetch=3,
+            grid=(slot_count // span,),
+            in_specs=[pl.BlockSpec((span, size, size), lambda s, *_: (s, 0, 0))],
+            out_specs=pl.BlockSpec((side * size, wide * size), lambda s, *_: (0, 0)),
+            scratch_shapes=[pltpu.VMEM((side * wide + 1, size, size), jnp.float32)],
+        ),
+        compiler_params=pltpu.CompilerParams(vmem_limit_bytes=48 * 2**20),
+        cost_estimate=pl.CostEstimate(
+            flops=slot_count * size * size * 40, bytes_accessed=4 * slot_count * size * size, transcendentals=0
+        ),
+        name="dense_cell",
+    )(live_count, out_local, in_local, cell_tiles)
+
+
+def layer_kernel(
+    R, C, S, factor,
+    a_ref, p_ref, feat_ref, w_ref, bias_ref, cot_ref,
+    out_ref, gfeat_ref, gw_ref, gb_ref,
+    part_send, part_recv, own, grads, gsum, back_send, back_recv, back_own,
+    w_send, w_recv, wr_recv, wc_recv,
+    s1, r1, s2, r2, s3, r3, s4, r4, s5, r5, s6, r6,
+):
+    my_row = lax.axis_index("row")
+    my_col = lax.axis_index("col")
+    n, d = feat_ref.shape
+    hb = n // S
+    f32, bf16 = jnp.float32, jnp.bfloat16
+    barrier = pltpu.get_barrier_semaphore()
+
+    def row_of(m):
+        return lax.rem(my_row + m, R)
+
+    def col_of(m):
+        return lax.rem(my_col + m, C)
+
+    for m in range(1, R):
+        pl.semaphore_signal(barrier, inc=1, device_id={"row": row_of(m)}, device_id_type=MESH)
+    for m in range(1, C):
+        pl.semaphore_signal(barrier, inc=1, device_id={"col": col_of(m)}, device_id_type=MESH)
+
+    def remote(src, dst, send, recv, where):
+        return pltpu.make_async_remote_copy(
+            src_ref=src, dst_ref=dst, send_sem=send, recv_sem=recv, device_id=where, device_id_type=MESH
+        )
+
+    sent = []
+    order = [2, 1, 3] if R == 4 else list(range(1, R))
+    corder = [2, 3, 1] if C == 4 else list(range(1, C))
+    first = [None] * (R * S)
+    waited = False
+    for h in range(S):
+        for m in order + [0]:
+            start = pl.multiple_of(row_of(m) * n + h * hb, hb)
+            total = jnp.dot(a_ref[pl.ds(start, hb), :], p_ref[...], preferred_element_type=f32)
+            if m == 0:
+                own[h] = total
+                continue
+            part_send[m - 1, h] = total.astype(bf16)
+            if not waited:
+                pl.semaphore_wait(barrier, R + C - 2)
+                waited = True
+            copy = remote(
+                part_send.at[m - 1, h], part_recv.at[m - 1, h],
+                s1.at[m - 1, h], r1.at[m - 1, h], {"row": row_of(m)},
+            )
+            copy.start()
+            sent.append(copy)
+            first[m * S + h] = copy
+
+    gbias = jnp.zeros((1, d), f32)
+    second = {}
+    for h in range(S):
+        rows = pl.ds(h * hb, hb)
+        hidden = own[h] + bias_ref[...]
+        for m in [1, 3, 2] if R == 4 else range(1, R):
+            first[m * S + h].wait_recv()
+            hidden = hidden + part_recv[m - 1, h].astype(f32)
+        gate = jax.nn.sigmoid(hidden)
+        g = cot_ref[rows, :].astype(f32) * gate * (1.0 + hidden * (1.0 - gate))
+        g = g.astype(bf16).astype(f32)
+        grads[0, h] = g.T.astype(bf16)
+        for m in order:
+            copy = remote(
+                grads.at[0, h], grads.at[m, h], s2.at[m - 1, h], r2.at[m - 1, h], {"row": row_of(m)}
+            )
+            copy.start()
+            sent.append(copy)
+            second[m, h] = copy
+        out_ref[rows, :] = (hidden * gate).astype(bf16)
+        gbias = gbias + jnp.sum(g, axis=0, keepdims=True)
+
+    steps = [(0, h) for h in range(S)]
+    steps += [(m, h) for h in range(S) for m in ([1, 3, 2] if R == 4 else range(1, R))]
+    third = {}
+    for at, (m, h) in enumerate(steps):
+        if m:
+            second[m, h].wait_recv()
+        start = pl.multiple_of(lax.rem(my_row + R - m, R) * n + h * hb, hb)
+        for k in corder + [0]:
+            c0 = pl.multiple_of(col_of(k) * n, n)
+            new = jnp.dot(
+                grads[m, h], a_ref[pl.ds(start, hb), pl.ds(c0, n)], preferred_element_type=f32
+            )
+            if at:
+                new = gsum[k] + new
+            if at < len(steps) - 1:
+                gsum[k] = new
+            elif k == 0:
+                gsum[0] = new
+            else:
+                back_send[k - 1] = new.astype(bf16)
+                copy = remote(
+                    back_send.at[k - 1], back_recv.at[k - 1], s3.at[k - 1], r3.at[k - 1], {"col": col_of(k)}
+                )
+                copy.start()
+                sent.append(copy)
+                third[k] = copy
+
+    total = gsum[0]
+    for k in [1, 2, 3] if C == 4 else range(1, C):
+        third[k].wait_recv()
+        total = total + back_recv[k - 1].astype(f32)
+    gproj = total.astype(bf16)
+    gweight = jnp.dot(gproj, feat_ref[...], preferred_element_type=f32).T * factor
+    gbias = gbias * factor
+    q = d // C
+    for k in range(C):
+        w_send[k, 0:q] = gweight[k * q : (k + 1) * q].astype(bf16)
+        w_send[k, q : q + 16] = jnp.broadcast_to(gbias, (16, d)).astype(bf16)
+    fourth = []
+    for k in corder:
+        copy = remote(
+            w_send.at[col_of(k)], w_recv.at[my_col], s4.at[k - 1], r4.at[k - 1], {"col": col_of(k)}
+        )
+        copy.start()
+        fourth.append(copy)
+    w_recv[my_col] = w_send[my_col]
+    back_own[...] = jnp.dot(w_ref[...], gproj, preferred_element_type=f32)
+    gfeat_ref[...] = back_own[...].T.astype(bf16)
+    for copy in fourth:
+        copy.wait_recv()
+    part = w_recv[0].astype(f32)
+    for k in range(1, C):
+        part = part + w_recv[k].astype(f32)
+    wr_recv[my_row] = part.astype(bf16)
+    fifth = []
+    for m in order:
+        copy = remote(
+            wr_recv.at[my_row], wr_recv.at[my_row], s5.at[m - 1], r5.at[m - 1], {"row": row_of(m)}
+        )
+        copy.start()
+        fifth.append(copy)
+    for copy in fifth:
+        copy.wait_recv()
+    part = wr_recv[0].astype(f32)
+    for m in range(1, R):
+        part = part + wr_recv[m].astype(f32)
+    gb_ref[...] = part[q : q + 1]
+    wc_recv[my_col] = part[0:q].astype(bf16)
+    sixth = []
+    for k in corder:
+        copy = remote(
+            wc_recv.at[my_col], wc_recv.at[my_col], s6.at[k - 1], r6.at[k - 1], {"col": col_of(k)}
+        )
+        copy.start()
+        sixth.append(copy)
+    for copy in sixth:
+        copy.wait_recv()
+    for k in range(C):
+        gw_ref[pl.ds(k * q, q), :] = wc_recv[k].astype(f32)
+    for copy in sent + fourth + fifth + sixth:
+        copy.wait_send()
+
+
+def dense_body(features, weight, bias, tiles, tile_out, tile_in, tile_count, cotangent):
+    slots, size = tiles.shape[2], tiles.shape[3]
+    n, d = features.shape
+    R, C = lax.axis_size("row"), lax.axis_size("col")
+    own = n // size
+    side, wide = own * R, own * C
+    projected = jnp.dot(features, weight, preferred_element_type=jnp.float32).astype(jnp.bfloat16)
+    dense = build_dense(
+        tiles.reshape(slots, size, size), tile_out.reshape(slots), tile_in.reshape(slots),
+        tile_count.reshape(1), side, wide,
+    )
+    me = lax.axis_index("col")
+    inputs = jnp.zeros((wide * size, d), jnp.bfloat16)
+    inputs = lax.dynamic_update_slice(inputs, projected, (me * n, 0))
+    for m in range(1, C):
+        got = lax.ppermute(projected, "col", [(c, (c + m) % C) for c in range(C)])
+        inputs = lax.dynamic_update_slice(inputs, got, ((me + C - m) % C * n, 0))
+    S = 2
+    hb = n // S
+    q = d // C
+    bf16, f32 = jnp.bfloat16, jnp.float32
+    vm = pl.BlockSpec(memory_space=pltpu.VMEM)
+    dma = pltpu.SemaphoreType.DMA
+    output, gfeat, gw, gb = pl.pallas_call(
+        functools.partial(layer_kernel, R, C, S, 1.0 / math.sqrt(n * R * C)),
+        out_shape=(
+            jax.ShapeDtypeStruct((n, d), bf16),
+            jax.ShapeDtypeStruct((n, d), bf16),
+            jax.ShapeDtypeStruct((d, d), f32),
+            jax.ShapeDtypeStruct((1, d), f32),
+        ),
+        in_specs=[vm] * 6,
+        out_specs=(vm,) * 4,
+        scratch_shapes=[
+            pltpu.VMEM((R - 1, S, hb, d), bf16),
+            pltpu.VMEM((R - 1, S, hb, d), bf16),
+            pltpu.VMEM((S, hb, d), f32),
+            pltpu.VMEM((R, S, d, hb), bf16),
+            pltpu.VMEM((C, d, n), f32),
+            pltpu.VMEM((C - 1, d, n), bf16),
+            pltpu.VMEM((C - 1, d, n), bf16),
+            pltpu.VMEM((d, n), f32),
+            pltpu.VMEM((C, q + 16, d), bf16),
+            pltpu.VMEM((C, q + 16, d), bf16),
+            pltpu.VMEM((R, q + 16, d), bf16),
+            pltpu.VMEM((C, q, d), bf16),
+            dma((R - 1, S)), dma((R - 1, S)), dma((R - 1, S)), dma((R - 1, S)),
+            dma((C - 1,)), dma((C - 1,)), dma((C - 1,)), dma((C - 1,)),
+            dma((R - 1,)), dma((R - 1,)), dma((C - 1,)), dma((C - 1,)),
+        ],
+        compiler_params=pltpu.CompilerParams(
+            collective_id=0, has_side_effects=True, vmem_limit_bytes=40 * 2**20
+        ),
+        cost_estimate=pl.CostEstimate(
+            flops=4 * n * R * n * C * d, bytes_accessed=2 * n * R * n * C, transcendentals=n * d
+        ),
+        name="layer",
+    )(dense, inputs, features, weight, bias.reshape(1, d), cotangent)
+    return output, gfeat, gw, gb.reshape(d)
+
+
+def layer_body(features, *rest):
+    cells = lax.axis_size("row") * lax.axis_size("col")
+    small = features.shape[0] * features.shape[0] * cells <= 2**22
+    return (dense_body if small else body)(features, *rest)
+
 
 def solution(mesh):
     placed = (
@@ -118,7 +401,7 @@
         P(("parts", "row", "col"), None),
     )
     return jax.shard_map(
-        body,
+        layer_body,
         mesh=mesh,
         in_specs=placed,
         out_specs=(

time: 390 us -> 101 us (0.26)
  waiting for transfers between devices: 216 us -> 0.01 us
  Pallas kernels: 0 us -> 85.8 us
  blocking collectives: 73.7 us -> 0 us
  matrix products: 38.2 us -> 1.22 us
  local copies, waits for them, and re-layouts: 38.6 us -> 7.56 us
  between operations: 14.5 us -> 1.41 us
  other arithmetic: 7.55 us -> 0 us
  starting transfers between devices: 0.21 us -> 4.46 us
    reduce_scatter x2 -> x0, waiting for transfers between devices: 92.6 us -> none  [the longest x1 89.8 us: body(): summed = lax.psum_scatter(partials, 'row', scatter_dimension=0, tiled=True)]
    psum x1 -> x0, waiting for transfers between devices: 88.6 us -> none  [body(): lax.psum((local_weight, local_bias), ('row', 'col'))]
    pallas_call x0 -> x2, Pallas kernels: none -> 85.8 us  [the longest x1 72.6 us: dense_body(): pl.pallas_call(functools.partial(layer_kernel, R, C, S, 1.0 / math.sqrt(n...]
    psum x1 -> x0, blocking collectives: 73.7 us -> none  [body(): lax.psum((local_weight, local_bias), ('row', 'col'))]
    dot_general x21 -> x1, matrix products: 38.2 us -> 1.22 us  [dense_body(): jnp.dot(features, weight, preferred_element_type=jnp.float32)]
    all_gather x2 -> x0, waiting for transfers between devices: 34.2 us -> none  [the longest x1 18.9 us: body(): inputs = lax.all_gather(projected, 'col', axis=0, tiled=True)]
    while x12 -> x0, local copies, waits for them, and re-layouts: 17.5 us -> none
    another operation x6 -> x0, local copies, waits for them, and re-layouts: 6.41 us -> none  [the longest x2 3.1 us: accumulate(): flat_source = source.reshape(from_count, cluster_size * feat_width)]
  transfers between devices with their start and end apart: 5 -> 3, of which waited for: 5 -> 0; matrix products, arithmetic and copies ran while one was open for 4% -> 0% of each run, Pallas kernels for 0% -> 13%
where the time goes in v1:
time: 101 us; the launch traced here: 100 us
  Pallas kernels  85.8 us (85%)
  local copies, waits for them, and re-layouts  7.56 us (7%)
  starting transfers between devices  4.46 us (4%)
  between operations  1.41 us (1%)
  matrix products  1.22 us (1%)
    pallas_call x1, Pallas kernels, dense_body(): pl.pallas_call(functools.partial(layer_kernel, R, C, S, 1.0 / math.sqrt(n...  72.6 us
    pallas_call x1, Pallas kernels, build_dense(): pl.pallas_call(build_kernel, out_shape=jax.ShapeDtypeStruct((side * size,...  13.2 us
    unnamed x18, local copies, waits for them, and re-layouts  7.41 us
    ppermute x3, starting transfers between devices, dense_body(): got = lax.ppermute(projected, 'col', [(c, (c + m) % C) for c in range(C)])  4.46 us
  transfers between devices with their start and end apart: 3, of which 0 were waited for; matrix products, arithmetic and copies ran while one was open for 0% of the time, Pallas kernels for 13%

profile of v1, /device:TPU:0, one launch (start us, length us, event | category | flops | bytes accessed | tf_op | source)
XLA Modules:
  0.0 100.5 jit_solution(13894702022236092031)
XLA Ops:
  0.6 0.1 broadcast_in_dim.3
  0.7 1.2 %constant_dynamic-update-slice_fusion.3 = (bf16[2048,256]{1,0:T(8,128)(2,1)S(1)}, bf16[512,256]{1,0:T(8,128)(2,1)S(1)}) fusion(bf16[2048,256]{1,0:T(8,128)(2,1)S(1)} %broadcast_in_dim.3, s32[]{:T(128)S(6)} %select_n.27, bf16[512,256]{1,0:T(8,128)(2,1)} %feat_ref.1, bf16[256,256]{1,0:T(8,128)(2,1)} %w_ref.1), kind=kOutput, calls=%fused_computation.4 | convolution fusion | flops 67239936 | bytes 917508 | tf_op jit(solution)/shard_map/dot_general | solution.py:331
  1.9 0.5 collective-permute-start
  2.4 2.6 %collective-permute-start.1 = (bf16[512,256]{1,0:T(8,128)(2,1)S(1)}, bf16[512,256]{1,0:T(8,128)(2,1)S(1)}, u32[]{:S(2)}, u32[]{:S(2)}) collective-permute-start(bf16[512,256]{1,0:T(8,128)(2,1)S(1)} %get-tuple-element.13), channel_id=1, source_target_pairs={{0,2},{1,3},{2,0},{3,1},{4,6},{5,7},{6,4},{7,5},{8,10},{9,11},{10,... | collective-permute-start | bytes 786440 | tf_op jit(solution)/shard_map/ppermute | solution.py:340
  5.0 1.4 %collective-permute-start.2 = (bf16[512,256]{1,0:T(8,128)(2,1)S(1)}, bf16[512,256]{1,0:T(8,128)(2,1)S(1)}, u32[]{:S(2)}, u32[]{:S(2)}) collective-permute-start(bf16[512,256]{1,0:T(8,128)(2,1)S(1)} %get-tuple-element.13), channel_id=1, source_target_pairs={{0,3},{1,0},{2,1},{3,2},{4,7},{5,4},{6,5},{7,6},{8,11},{9,8},{10,9... | collective-permute-start | bytes 786440 | tf_op jit(solution)/shard_map/ppermute | solution.py:340
  7.1 0.0 copy-start.3
  7.1 0.7 copy-done.3
  7.7 0.0 copy-start.4
  7.7 0.7 copy-done.4
  8.4 0.0 copy-start.1
  8.4 0.0 copy-start.2
  8.4 0.0 copy-start.5
  8.4 0.0 copy-start.6
  8.4 13.2 %dense_cell.1.a_ref = bf16[2048,2048]{1,0:T(8,128)(2,1)} custom-call(s32[1]{0:T(128)} %bitcast.8.count_ref, s32[256]{0:T(256)S(1)} %bitcast.10, s32[256]{0:T(256)S(1)} %bitcast.11, bf16[256,128,128]{2,1,0:T(8,128)(2,1)} %bitcast.13), custom_call_target="tpu_custom_call" | custom-call | flops 167772160 | bytes 16777216 | tf_op jit(solution)/shard_map/dense_cell/pallas_call | solution.py:147
  21.6 0.0 collective-permute-done
  21.6 0.0 collective-permute-done.1
  21.7 0.0 collective-permute-done.2
  21.7 0.0 copy-done.1
  21.7 0.0 copy-done.2
  21.7 0.0 copy-done.5
  21.7 0.0 copy-done.6
  21.7 0.0 copy-start
  21.7 3.4 %copy-done = bf16[2048,2048]{1,0:T(8,128)(2,1)S(1)} copy-done((bf16[2048,2048]{1,0:T(8,128)(2,1)S(1)}, bf16[2048,2048]{1,0:T(8,128)(2,1)}, u32[]{:S(2)}) %copy-start) | copy-done | bytes 8388632
  25.1 72.6 %layer.1 = (bf16[512,256]{1,0:T(8,128)(2,1)S(1)}, bf16[512,256]{1,0:T(8,128)(2,1)S(1)}, f32[256,256]{1,0:T(8,128)S(1)}, f32[1,256]{1,0:T(1,128)S(1)}) custom-call(bf16[2048,2048]{1,0:T(8,128)(2,1)S(1)} %copy-done, bf16[2048,256]{1,0:T(8,128)(2,1)S(1)} %constant_dynamic-update-slice_fusion.p_ref, bf16[512,256]{1,0:T(8,128)(2,1)S(1)} %copy-done.1, ...), custom_call_target="tpu_custom_call" | custom-call | flops 4294967296 | bytes 8388608 | tf_op jit(solution)/shard_map/layer/pallas_call | solution.py:348
  97.8 0.7 copy.21
  98.5 0.7 copy.22
  99.2 0.7 copy.23
  99.9 0.6 copy.24
  (3 shorter events, 0.1 us)
Async XLA Ops:
  1.9 19.6 %collective-permute-start = (bf16[512,256]{1,0:T(8,128)(2,1)S(1)}, bf16[512,256]{1,0:T(8,128)(2,1)S(1)}, u32[]{:S(2)}, u32[]{:S(2)}) collective-permute-start(bf16[512,256]{1,0:T(8,128)(2,1)S(1)} %get-tuple-element.13), channel_id=1, source_target_pairs={{0,1},{1,2},{2,3},{3,0},{4,5},{5,6},{6,7},{7,4},{8,9},{9,10},{10,1... | collective-permute-start | bytes 786440 | tf_op jit(solution)/shard_map/ppermute | solution.py:340
  2.4 19.2 %collective-permute-start.1 = (bf16[512,256]{1,0:T(8,128)(2,1)S(1)}, bf16[512,256]{1,0:T(8,128)(2,1)S(1)}, u32[]{:S(2)}, u32[]{:S(2)}) collective-permute-start(bf16[512,256]{1,0:T(8,128)(2,1)S(1)} %get-tuple-element.13), channel_id=1, source_target_pairs={{0,2},{1,3},{2,0},{3,1},{4,6},{5,7},{6,4},{7,5},{8,10},{9,11},{10,... | collective-permute-start | bytes 786440 | tf_op jit(solution)/shard_map/ppermute | solution.py:340
  5.0 16.6 %collective-permute-start.2 = (bf16[512,256]{1,0:T(8,128)(2,1)S(1)}, bf16[512,256]{1,0:T(8,128)(2,1)S(1)}, u32[]{:S(2)}, u32[]{:S(2)}) collective-permute-start(bf16[512,256]{1,0:T(8,128)(2,1)S(1)} %get-tuple-element.13), channel_id=1, source_target_pairs={{0,3},{1,0},{2,1},{3,2},{4,7},{5,4},{6,5},{7,6},{8,11},{9,8},{10,9... | collective-permute-start | bytes 786440 | tf_op jit(solution)/shard_map/ppermute | solution.py:340
  7.1 0.7 copy-start.3
  7.7 0.7 copy-start.4
  8.4 13.3 %copy-start.1 = (bf16[512,256]{1,0:T(8,128)(2,1)S(1)}, bf16[512,256]{1,0:T(8,128)(2,1)}, u32[]{:S(2)}) copy-start(bf16[512,256]{1,0:T(8,128)(2,1)} %feat_ref.1) | copy-start | bytes 786436
  8.4 13.3 %copy-start.2 = (bf16[256,256]{1,0:T(8,128)(2,1)S(1)}, bf16[256,256]{1,0:T(8,128)(2,1)}, u32[]{:S(2)}) copy-start(bf16[256,256]{1,0:T(8,128)(2,1)} %w_ref.1) | copy-start | bytes 393220
  8.4 13.3 %copy-start.5 = (bf16[512,256]{1,0:T(8,128)(2,1)S(1)}, bf16[512,256]{1,0:T(8,128)(2,1)}, u32[]{:S(2)}) copy-start(bf16[512,256]{1,0:T(8,128)(2,1)} %cot_ref.1) | copy-start | bytes 786436
  8.4 13.3 %copy-start.6 = (f32[256]{0:T(256)S(1)}, f32[256]{0:T(256)}, u32[]{:S(2)}) copy-start(f32[256]{0:T(256)} %param.10) | copy-start | bytes 3076
  21.7 3.4 %copy-start = (bf16[2048,2048]{1,0:T(8,128)(2,1)S(1)}, bf16[2048,2048]{1,0:T(8,128)(2,1)}, u32[]{:S(2)}) copy-start(bf16[2048,2048]{1,0:T(8,128)(2,1)} %dense_cell.1.a_ref) | copy-start | bytes 25165828

commit v2 on v1

--- a/solution.py
+++ b/solution.py
@@ -110,51 +110,73 @@
     factor = 1.0 / math.sqrt(own_rows * row_devices * col_devices)
     return (output, grad_features, grad_weight * factor, grad_bias * factor)
 
-def build_kernel(count_ref, out_ids, in_ids, tiles_ref, dense_ref, sums):
-    step = pl.program_id(0)
-    slots, size = tiles_ref.shape[0], tiles_ref.shape[1]
-    side = dense_ref.shape[0] // size
-    wide = dense_ref.shape[1] // size
+def build_kernel(count_ref, out_ids, in_ids, tiles_hbm, dense_hbm, sums, held, dense, in_sem, out_sem):
+    slots, size = held.shape[0], held.shape[1]
+    side = dense.shape[0] // size
+    wide = dense.shape[1] // size
     spare = side * wide
-
-    @pl.when(step == 0)
-    def _():
-        sums[...] = jnp.zeros_like(sums)
-
-    def add(slot, _):
-        where = step * slots + slot
+    spans = in_sem.shape[0]
+    span = slots // spans
+
+    def fetch(step):
+        part = pl.ds(step * span, span)
+        return pltpu.make_async_copy(tiles_hbm.at[part], held.at[part], in_sem.at[step])
+
+    for step in range(spans):
+        fetch(step).start()
+
+    def clear(at, _):
+        sums[at] = jnp.zeros_like(sums[0])
+        return 0
+
+    lax.fori_loop(0, spare, clear, 0, unroll=8)
+
+    def add(where, _):
         pair = out_ids[where] * wide + in_ids[where]
         pair = jnp.where(where < count_ref[0], pair, spare)
-        sums[pair] += tiles_ref[slot].astype(jnp.float32)
+        sums[pair] += held[where].astype(jnp.float32)
         return 0
 
-    lax.fori_loop(0, slots, add, 0, unroll=8)
-
-    @pl.when(step == pl.num_programs(0) - 1)
-    def _():
-        def write(o, _):
-            rows = pl.ds(pl.multiple_of(o * size, size), size)
-            for i in range(wide):
-                dense_ref[rows, pl.ds(i * size, size)] = sums[o * wide + i].astype(jnp.bfloat16)
-            return 0
-
-        lax.fori_loop(0, side, write, 0)
+    for step in range(spans):
+        fetch(step).wait()
+        lax.fori_loop(step * span, (step + 1) * span, add, 0, unroll=8)
+
+    def put(o):
+        rows = pl.ds(pl.multiple_of(o * size, size), size)
+        return pltpu.make_async_copy(dense.at[rows], dense_hbm.at[rows], out_sem.at[o])
+
+    def write(o, _):
+        rows = pl.ds(pl.multiple_of(o * size, size), size)
+        for i in range(wide):
+            dense[rows, pl.ds(i * size, size)] = sums[o * wide + i].astype(jnp.bfloat16)
+        put(o).start()
+        return 0
+
+    lax.fori_loop(0, side, write, 0)
+    for o in range(side):
+        put(o).wait()
 
 
 def build_dense(cell_tiles, out_local, in_local, live_count, side, wide):
     slot_count, size, _ = cell_tiles.shape
-    span = 32
+    spans = 8
     return pl.pallas_call(
         build_kernel,
         out_shape=jax.ShapeDtypeStruct((side * size, wide * size), jnp.bfloat16),
         grid_spec=pltpu.PrefetchScalarGridSpec(
             num_scalar_prefetch=3,
-            grid=(slot_count // span,),
-            in_specs=[pl.BlockSpec((span, size, size), lambda s, *_: (s, 0, 0))],
-            out_specs=pl.BlockSpec((side * size, wide * size), lambda s, *_: (0, 0)),
-            scratch_shapes=[pltpu.VMEM((side * wide + 1, size, size), jnp.float32)],
+            grid=(1,),
+            in_specs=[pl.BlockSpec(memory_space=pl.ANY)],
+            out_specs=pl.BlockSpec(memory_space=pl.ANY),
+            scratch_shapes=[
+                pltpu.VMEM((side * wide + 1, size, size), jnp.float32),
+                pltpu.VMEM((slot_count, size, size), jnp.bfloat16),
+                pltpu.VMEM((side * size, wide * size), jnp.bfloat16),
+                pltpu.SemaphoreType.DMA((spans,)),
+                pltpu.SemaphoreType.DMA((side,)),
+            ],
         ),
-        compiler_params=pltpu.CompilerParams(vmem_limit_bytes=48 * 2**20),
+        compiler_params=pltpu.CompilerParams(vmem_limit_bytes=56 * 2**20),
         cost_estimate=pl.CostEstimate(
             flops=slot_count * size * size * 40, bytes_accessed=4 * slot_count * size * size, transcendentals=0
         ),
@@ -164,11 +186,11 @@
 
 def layer_kernel(
     R, C, S, factor,
-    a_ref, p_ref, feat_ref, w_ref, bias_ref, cot_ref,
+    a_hbm, p_ref, feat_ref, w_ref, bias_ref, cot_ref,
     out_ref, gfeat_ref, gw_ref, gb_ref,
-    part_send, part_recv, own, grads, gsum, back_send, back_recv, back_own,
+    a_ref, part, part_send, part_recv, hid, grads, gsum, back_send, back_recv, back_own,
     w_send, w_recv, wr_recv, wc_recv,
-    s1, r1, s2, r2, s3, r3, s4, r4, s5, r5, s6, r6,
+    a_sem, s1, r1, s2, s2b, r2, s3, r3, s4, r4, s5, r5, s6, r6,
 ):
     my_row = lax.axis_index("row")
     my_col = lax.axis_index("col")
@@ -193,83 +215,150 @@
             src_ref=src, dst_ref=dst, send_sem=send, recv_sem=recv, device_id=where, device_id_type=MESH
         )
 
-    sent = []
-    order = [2, 1, 3] if R == 4 else list(range(1, R))
-    corder = [2, 3, 1] if C == 4 else list(range(1, C))
-    first = [None] * (R * S)
-    waited = False
+    order = [2, 1, 3]
+    corder = [2, 3, 1]
+
+    high = my_row // 2
+    place = (1 - high) * my_row + high * (R - 1 - my_row)
+
+    def at(p):
+        return (1 - high) * p + high * (R - 1 - p)
+
+    pair_row = at(1 - place)
+    next_row = at(place + 1)
+    inner_row = at(2)
+    outer, inner = place == 0, place == 1
+
+    targets = [at(3), at(2), pair_row, my_row]
+    fetches = []
+    for k in range(R):
+        rows = pl.ds(pl.multiple_of(targets[k] * n, n), n)
+        fetches.append(pltpu.make_async_copy(a_hbm.at[rows], a_ref.at[rows], a_sem.at[k]))
+        fetches[k].start()
+
+    def sum_to_pair(k, h):
+        return remote(
+            part_send.at[k, h], part_recv.at[k, h], s1.at[k, h], r1.at[k, h], {"row": pair_row}
+        )
+
+    def sum_to_inner(k, h):
+        return remote(
+            part_send.at[k, h], part_recv.at[k + 3, h], s1.at[k, h], r1.at[k + 3, h], {"row": inner_row}
+        )
+
+    pl.semaphore_wait(barrier, R + C - 2)
     for h in range(S):
-        for m in order + [0]:
-            start = pl.multiple_of(row_of(m) * n + h * hb, hb)
-            total = jnp.dot(a_ref[pl.ds(start, hb), :], p_ref[...], preferred_element_type=f32)
-            if m == 0:
-                own[h] = total
-                continue
-            part_send[m - 1, h] = total.astype(bf16)
-            if not waited:
-                pl.semaphore_wait(barrier, R + C - 2)
-                waited = True
-            copy = remote(
-                part_send.at[m - 1, h], part_recv.at[m - 1, h],
-                s1.at[m - 1, h], r1.at[m - 1, h], {"row": row_of(m)},
+        for k in range(R):
+            if h == 0:
+                fetches[k].wait()
+            start = pl.multiple_of(targets[k] * n + h * hb, hb)
+            part[k, h] = jnp.dot(a_ref[pl.ds(start, hb), :], p_ref[...], preferred_element_type=f32)
+            if k < 3:
+
+                @pl.when(outer)
+                def _():
+                    part_send[k, h] = part[k, h].astype(bf16)
+                    sum_to_pair(k, h).start()
+
+    def grad_to_pair(p, h, sem):
+        row = at(p)
+        return remote(grads.at[row, h], grads.at[row, h], sem, r2.at[row, h], {"row": pair_row})
+
+    def grad_to_inner(p, h, sem):
+        row = at(p)
+        return remote(grads.at[row, h], grads.at[row, h], sem, r2.at[row, h], {"row": inner_row})
+
+    gbias = jnp.zeros((1, d), f32)
+    own_cols = [3, 2, 1, 0]
+
+    def col_block(k):
+        chip, core = my_col // 2, lax.rem(my_col, 2)
+        chip = 1 - chip if k >= 2 else chip
+        core = 1 - core if k % 2 else core
+        return chip * 2 + core
+
+    def back(p, h, first, last):
+        row = at(p)
+        start = pl.multiple_of(row * n + h * hb, hb)
+        for k in own_cols:
+            c0 = pl.multiple_of(col_block(k) * n, n)
+            new = jnp.dot(
+                grads[row, h], a_ref[pl.ds(start, hb), pl.ds(c0, n)], preferred_element_type=f32
             )
-            copy.start()
-            sent.append(copy)
-            first[m * S + h] = copy
-
-    gbias = jnp.zeros((1, d), f32)
-    second = {}
-    for h in range(S):
-        rows = pl.ds(h * hb, hb)
-        hidden = own[h] + bias_ref[...]
-        for m in [1, 3, 2] if R == 4 else range(1, R):
-            first[m * S + h].wait_recv()
-            hidden = hidden + part_recv[m - 1, h].astype(f32)
-        gate = jax.nn.sigmoid(hidden)
-        g = cot_ref[rows, :].astype(f32) * gate * (1.0 + hidden * (1.0 - gate))
-        g = g.astype(bf16).astype(f32)
-        grads[0, h] = g.T.astype(bf16)
-        for m in order:
-            copy = remote(
-                grads.at[0, h], grads.at[m, h], s2.at[m - 1, h], r2.at[m - 1, h], {"row": row_of(m)}
-            )
-            copy.start()
-            sent.append(copy)
-            second[m, h] = copy
-        out_ref[rows, :] = (hidden * gate).astype(bf16)
-        gbias = gbias + jnp.sum(g, axis=0, keepdims=True)
-
-    steps = [(0, h) for h in range(S)]
-    steps += [(m, h) for h in range(S) for m in ([1, 3, 2] if R == 4 else range(1, R))]
-    third = {}
-    for at, (m, h) in enumerate(steps):
-        if m:
-            second[m, h].wait_recv()
-        start = pl.multiple_of(lax.rem(my_row + R - m, R) * n + h * hb, hb)
-        for k in corder + [0]:
-            c0 = pl.multiple_of(col_of(k) * n, n)
-            new = jnp.dot(
-                grads[m, h], a_ref[pl.ds(start, hb), pl.ds(c0, n)], preferred_element_type=f32
-            )
-            if at:
+            if not first:
                 new = gsum[k] + new
-            if at < len(steps) - 1:
-                gsum[k] = new
-            elif k == 0:
-                gsum[0] = new
-            else:
-                back_send[k - 1] = new.astype(bf16)
-                copy = remote(
-                    back_send.at[k - 1], back_recv.at[k - 1], s3.at[k - 1], r3.at[k - 1], {"col": col_of(k)}
-                )
-                copy.start()
-                sent.append(copy)
-                third[k] = copy
-
-    total = gsum[0]
-    for k in [1, 2, 3] if C == 4 else range(1, C):
-        third[k].wait_recv()
-        total = total + back_recv[k - 1].astype(f32)
+            gsum[k] = new
+            if last and k in (3, 1):
+                back_send[k] = new.astype(bf16)
+                back_copy(k).start()
+
+    def back_copy(k):
+        if k == 2:
+            return remote(back_send.at[2], back_recv.at[2], s3.at[2], r3.at[2], {"col": col_block(2)})
+        return remote(back_send.at[k], back_recv.at[k], s3.at[k], r3.at[k], {"col": col_block(1)})
+
+    for h in range(S + 1):
+        if h < S:
+
+            @pl.when(inner)
+            def _():
+                for k in range(3):
+                    if k < 2:
+                        sum_to_pair(k, h).wait_recv()
+                        got = part_recv[k, h]
+                    else:
+                        sum_to_inner(0, h).wait_recv()
+                        got = part_recv[3, h]
+                    part_send[k, h] = (part[k, h] + got.astype(f32)).astype(bf16)
+                    if k < 2:
+                        sum_to_inner(k, h).start()
+                    else:
+                        sum_to_pair(k, h).start()
+
+            rows = pl.ds(h * hb, hb)
+            sum_to_pair(2, h).wait_recv()
+            hid[...] = part[3, h] + bias_ref[...] + part_recv[2, h].astype(f32)
+
+            @pl.when(inner)
+            def _():
+                sum_to_inner(1, h).wait_recv()
+                hid[...] += part_recv[4, h].astype(f32)
+
+            hidden = hid[...]
+            gate = jax.nn.sigmoid(hidden)
+            g = cot_ref[rows, :].astype(f32) * gate * (1.0 + hidden * (1.0 - gate))
+            g = g.astype(bf16).astype(f32)
+            grads[my_row, h] = g.T.astype(bf16)
+            grad_to_pair(place, h, s2.at[0, h]).start()
+
+            @pl.when(inner)
+            def _():
+                grad_to_inner(place, h, s2b.at[0, h]).start()
+
+            out_ref[rows, :] = (hidden * gate).astype(bf16)
+            gbias = gbias + jnp.sum(g, axis=0, keepdims=True)
+        if h > 0:
+            e = h - 1
+            back(place, e, e == 0, False)
+            for j, p in enumerate([1 - place, 2, 3]):
+                grad_to_pair(p, e, s2.at[0, e]).wait_recv()
+
+                @pl.when(inner)
+                def _():
+                    if j == 0:
+                        grad_to_inner(p, e, s2b.at[1, e]).start()
+                    else:
+                        grad_to_pair(p, e, s2.at[j, e]).start()
+
+                back(p, e, False, e == S - 1 and j == 2)
+
+    back_copy(3).wait_recv()
+    back_send[2] = (gsum[2] + back_recv[3].astype(f32)).astype(bf16)
+    back_copy(2).start()
+    back_copy(1).wait_recv()
+    total = gsum[0] + back_recv[1].astype(f32)
+    back_copy(2).wait_recv()
+    total = total + back_recv[2].astype(f32)
     gproj = total.astype(bf16)
     gweight = jnp.dot(gproj, feat_ref[...], preferred_element_type=f32).T * factor
     gbias = gbias * factor
@@ -289,10 +378,10 @@
     gfeat_ref[...] = back_own[...].T.astype(bf16)
     for copy in fourth:
         copy.wait_recv()
-    part = w_recv[0].astype(f32)
+    both = w_recv[0].astype(f32)
     for k in range(1, C):
-        part = part + w_recv[k].astype(f32)
-    wr_recv[my_row] = part.astype(bf16)
+        both = both + w_recv[k].astype(f32)
+    wr_recv[my_row] = both.astype(bf16)
     fifth = []
     for m in order:
         copy = remote(
@@ -302,11 +391,11 @@
         fifth.append(copy)
     for copy in fifth:
         copy.wait_recv()
-    part = wr_recv[0].astype(f32)
+    both = wr_recv[0].astype(f32)
     for m in range(1, R):
-        part = part + wr_recv[m].astype(f32)
-    gb_ref[...] = part[q : q + 1]
-    wc_recv[my_col] = part[0:q].astype(bf16)
+        both = both + wr_recv[m].astype(f32)
+    gb_ref[...] = both[q : q + 1]
+    wc_recv[my_col] = both[0:q].astype(bf16)
     sixth = []
     for k in corder:
         copy = remote(
@@ -318,8 +407,21 @@
         copy.wait_recv()
     for k in range(C):
         gw_ref[pl.ds(k * q, q), :] = wc_recv[k].astype(f32)
-    for copy in sent + fourth + fifth + sixth:
+    for copy in fourth + fifth + sixth:
         copy.wait_send()
+    for k in range(1, C):
+        back_copy(k).wait_send()
+    for h in range(S):
+        for k in range(3):
+            sum_to_pair(k, h).wait_send()
+        grad_to_pair(place, h, s2.at[0, h]).wait_send()
+
+        @pl.when(inner)
+        def _():
+            grad_to_inner(place, h, s2b.at[0, h]).wait_send()
+            grad_to_inner(0, h, s2b.at[1, h]).wait_send()
+            grad_to_pair(2, h, s2.at[1, h]).wait_send()
+            grad_to_pair(3, h, s2.at[2, h]).wait_send()
 
 
 def dense_body(features, weight, bias, tiles, tile_out, tile_in, tile_count, cotangent):
@@ -339,7 +441,7 @@
     for m in range(1, C):
         got = lax.ppermute(projected, "col", [(c, (c + m) % C) for c in range(C)])
         inputs = lax.dynamic_update_slice(inputs, got, ((me + C - m) % C * n, 0))
-    S = 2
+    S = 4
     hb = n // S
     q = d // C
     bf16, f32 = jnp.bfloat16, jnp.float32
@@ -353,27 +455,29 @@
             jax.ShapeDtypeStruct((d, d), f32),
             jax.ShapeDtypeStruct((1, d), f32),
         ),
-        in_specs=[vm] * 6,
+        in_specs=[pl.BlockSpec(memory_space=pl.ANY)] + [vm] * 5,
         out_specs=(vm,) * 4,
         scratch_shapes=[
-            pltpu.VMEM((R - 1, S, hb, d), bf16),
-            pltpu.VMEM((R - 1, S, hb, d), bf16),
-            pltpu.VMEM((S, hb, d), f32),
+            pltpu.VMEM((R * n, C * n), bf16),
+            pltpu.VMEM((R, S, hb, d), f32),
+            pltpu.VMEM((3, S, hb, d), bf16),
+            pltpu.VMEM((5, S, hb, d), bf16),
+            pltpu.VMEM((hb, d), f32),
             pltpu.VMEM((R, S, d, hb), bf16),
             pltpu.VMEM((C, d, n), f32),
-            pltpu.VMEM((C - 1, d, n), bf16),
-            pltpu.VMEM((C - 1, d, n), bf16),
+            pltpu.VMEM((C, d, n), bf16),
+            pltpu.VMEM((C, d, n), bf16),
             pltpu.VMEM((d, n), f32),
             pltpu.VMEM((C, q + 16, d), bf16),
             pltpu.VMEM((C, q + 16, d), bf16),
             pltpu.VMEM((R, q + 16, d), bf16),
             pltpu.VMEM((C, q, d), bf16),
-            dma((R - 1, S)), dma((R - 1, S)), dma((R - 1, S)), dma((R - 1, S)),
-            dma((C - 1,)), dma((C - 1,)), dma((C - 1,)), dma((C - 1,)),
+            dma((R,)), dma((3, S)), dma((5, S)), dma((3, S)), dma((2, S)), dma((R, S)),
+            dma((C,)), dma((C,)), dma((C - 1,)), dma((C - 1,)),
             dma((R - 1,)), dma((R - 1,)), dma((C - 1,)), dma((C - 1,)),
         ],
         compiler_params=pltpu.CompilerParams(
-            collective_id=0, has_side_effects=True, vmem_limit_bytes=40 * 2**20
+            collective_id=0, has_side_effects=True, vmem_limit_bytes=58 * 2**20
         ),
         cost_estimate=pl.CostEstimate(
             flops=4 * n * R * n * C * d, bytes_accessed=2 * n * R * n * C, transcendentals=n * d
@@ -384,8 +488,7 @@
 
 
 def layer_body(features, *rest):
-    cells = lax.axis_size("row") * lax.axis_size("col")
-    small = features.shape[0] * features.shape[0] * cells <= 2**22
+    small = lax.axis_size("row") == 4 and lax.axis_size("col") == 4 and features.shape[0] == 512
     return (dense_body if small else body)(features, *rest)
 
 

time: 101 us -> 102 us (level)
  waiting for transfers between devices: 0.01 us -> 1.58 us
    pallas_call x1, Pallas kernels: 13.2 us -> 7.95 us  [build_dense(): pl.pallas_call(build_kernel, out_shape=jax.ShapeDtypeStruct((side * size,...]
    pallas_call x1, Pallas kernels: 72.6 us -> 77.4 us  [dense_body(): pl.pallas_call(functools.partial(layer_kernel, R, C, S, 1.0 / math.sqrt(n...]
    ppermute x3, waiting for transfers between devices: 0.01 us -> 1.58 us  [dense_body(): got = lax.ppermute(projected, 'col', [(c, (c + m) % C) for c in range(C)])]
    unnamed x18 -> x6, local copies, waits for them, and re-layouts: 7.41 us -> 7.22 us
  transfers between devices with their start and end apart: 3 -> 3, of which waited for: 0 -> 1; matrix products, arithmetic and copies ran while one was open for 0% -> 0% of each run, Pallas kernels for 13% -> 8%
where the time goes in v2:
time: 102 us; the launch traced here: 101 us
  Pallas kernels  85.3 us (84%)
  local copies, waits for them, and re-layouts  7.37 us (7%)
  starting transfers between devices  4.46 us (4%)
  waiting for transfers between devices  1.58 us (2%)
  between operations  1.37 us (1%)
  matrix products  1.22 us (1%)
    pallas_call x1, Pallas kernels, dense_body(): pl.pallas_call(functools.partial(layer_kernel, R, C, S, 1.0 / math.sqrt(n...  77.4 us
    pallas_call x1, Pallas kernels, build_dense(): pl.pallas_call(build_kernel, out_shape=jax.ShapeDtypeStruct((side * size,...  7.95 us
    unnamed x6, local copies, waits for them, and re-layouts  7.22 us
    ppermute x3, starting transfers between devices, dense_body(): got = lax.ppermute(projected, 'col', [(c, (c + m) % C) for c in range(C)])  4.46 us
  transfers between devices with their start and end apart: 3, of which 1 were waited for; matrix products, arithmetic and copies ran while one was open for 0% of the time, Pallas kernels for 8%

profile of v2, /device:TPU:0, one launch (start us, length us, event | category | flops | bytes accessed | tf_op | source)
XLA Modules:
  0.0 101.3 jit_solution(8631764242322692116)
XLA Ops:
  0.6 0.1 broadcast_in_dim.3
  0.7 1.2 %constant_dynamic-update-slice_fusion.3 = (bf16[2048,256]{1,0:T(8,128)(2,1)S(1)}, bf16[512,256]{1,0:T(8,128)(2,1)S(1)}) fusion(bf16[2048,256]{1,0:T(8,128)(2,1)S(1)} %broadcast_in_dim.3, s32[]{:T(128)S(6)} %select_n.27, bf16[512,256]{1,0:T(8,128)(2,1)} %feat_ref.1, bf16[256,256]{1,0:T(8,128)(2,1)} %w_ref.1), kind=kOutput, calls=%fused_computation.4 | convolution fusion | flops 67239936 | bytes 917508 | tf_op jit(solution)/shard_map/dot_general | solution.py:433
  1.9 0.5 collective-permute-start
  2.4 2.6 %collective-permute-start.1 = (bf16[512,256]{1,0:T(8,128)(2,1)S(1)}, bf16[512,256]{1,0:T(8,128)(2,1)S(1)}, u32[]{:S(2)}, u32[]{:S(2)}) collective-permute-start(bf16[512,256]{1,0:T(8,128)(2,1)S(1)} %get-tuple-element.13), channel_id=1, source_target_pairs={{0,2},{1,3},{2,0},{3,1},{4,6},{5,7},{6,4},{7,5},{8,10},{9,11},{10,... | collective-permute-start | bytes 786440 | tf_op jit(solution)/shard_map/ppermute | solution.py:442
  5.0 1.4 %collective-permute-start.2 = (bf16[512,256]{1,0:T(8,128)(2,1)S(1)}, bf16[512,256]{1,0:T(8,128)(2,1)S(1)}, u32[]{:S(2)}, u32[]{:S(2)}) collective-permute-start(bf16[512,256]{1,0:T(8,128)(2,1)S(1)} %get-tuple-element.13), channel_id=1, source_target_pairs={{0,3},{1,0},{2,1},{3,2},{4,7},{5,4},{6,5},{7,6},{8,11},{9,8},{10,9... | collective-permute-start | bytes 786440 | tf_op jit(solution)/shard_map/ppermute | solution.py:442
  7.1 7.9 %dense_cell.1.a_hbm = bf16[2048,2048]{1,0:T(8,128)(2,1)} custom-call(s32[1]{0:T(128)} %bitcast.8.count_ref, s32[256]{0:T(256)} %bitcast.11, s32[256]{0:T(256)} %bitcast.12, bf16[256,128,128]{2,1,0:T(8,128)(2,1)} %bitcast.9), custom_call_target="tpu_custom_call" | custom-call | flops 167772160 | bytes 16777216 | tf_op jit(solution)/shard_map/dense_cell/pallas_call | solution.py:163
  15.0 0.0 collective-permute-done
  15.1 0.0 collective-permute-done.1
  15.1 1.6 %collective-permute-done.2 = bf16[512,256]{1,0:T(8,128)(2,1)S(1)} collective-permute-done((bf16[512,256]{1,0:T(8,128)(2,1)S(1)}, bf16[512,256]{1,0:T(8,128)(2,1)S(1)}, u32[]{:S(2)}, u32[]{:S(2)}) %collective-permute-start.2) | collective-permute-done | bytes 262176 | tf_op jit(solution)/shard_map/ppermute | solution.py:442
  16.7 0.0 copy-start
  16.7 1.0 %copy-done = bf16[2048,256]{1,0:T(8,128)(2,1)} copy-done((bf16[2048,256]{1,0:T(8,128)(2,1)}, bf16[2048,256]{1,0:T(8,128)(2,1)S(1)}, u32[]{:S(2)}) %copy-start) | copy-done | bytes 1048600
  17.7 77.4 %layer.1 = (bf16[512,256]{1,0:T(8,128)(2,1)}, bf16[512,256]{1,0:T(8,128)(2,1)}, f32[256,256]{1,0:T(8,128)}, f32[1,256]{1,0:T(1,128)}) custom-call(bf16[2048,2048]{1,0:T(8,128)(2,1)} %dense_cell.1.a_hbm, bf16[2048,256]{1,0:T(8,128)(2,1)} %copy-done, bf16[512,256]{1,0:T(8,128)(2,1)} %feat_ref.1, bf16[256,256]{1,0:T(8,128)(2,1)} %w_ref.1, f32[1,256]{1,0:T(1,128)} %bitcast.13, ...), custom_call_target="tpu_custom_call" | custom-call | flops 4294967296 | bytes 8388608 | tf_op jit(solution)/shard_map/layer/pallas_call | solution.py:450
  95.1 1.7 %copy.21 = bf16[512,256]{1,0:T(8,128)(2,1)} copy(bf16[512,256]{1,0:T(8,128)(2,1)} %get-tuple-element.18) | data formatting | bytes 524288
  96.8 1.7 %copy.22 = bf16[512,256]{1,0:T(8,128)(2,1)} copy(bf16[512,256]{1,0:T(8,128)(2,1)} %get-tuple-element.19) | data formatting | bytes 524288
  98.5 1.7 %copy.23 = f32[256,256]{1,0:T(8,128)} copy(f32[256,256]{1,0:T(8,128)} %get-tuple-element.20) | data formatting | bytes 524288
  100.1 1.2 %copy.24 = f32[256]{0:T(256)} copy(f32[256]{0:T(256)} %bitcast.10) | data formatting | bytes 2048
  (3 shorter events, 0.1 us)
Async XLA Ops:
  1.9 13.1 %collective-permute-start = (bf16[512,256]{1,0:T(8,128)(2,1)S(1)}, bf16[512,256]{1,0:T(8,128)(2,1)S(1)}, u32[]{:S(2)}, u32[]{:S(2)}) collective-permute-start(bf16[512,256]{1,0:T(8,128)(2,1)S(1)} %get-tuple-element.13), channel_id=1, source_target_pairs={{0,1},{1,2},{2,3},{3,0},{4,5},{5,6},{6,7},{7,4},{8,9},{9,10},{10,1... | collective-permute-start | bytes 786440 | tf_op jit(solution)/shard_map/ppermute | solution.py:442
  2.4 12.6 %collective-permute-start.1 = (bf16[512,256]{1,0:T(8,128)(2,1)S(1)}, bf16[512,256]{1,0:T(8,128)(2,1)S(1)}, u32[]{:S(2)}, u32[]{:S(2)}) collective-permute-start(bf16[512,256]{1,0:T(8,128)(2,1)S(1)} %get-tuple-element.13), channel_id=1, source_target_pairs={{0,2},{1,3},{2,0},{3,1},{4,6},{5,7},{6,4},{7,5},{8,10},{9,11},{10,... | collective-permute-start | bytes 786440 | tf_op jit(solution)/shard_map/ppermute | solution.py:442
  5.0 11.7 %collective-permute-start.2 = (bf16[512,256]{1,0:T(8,128)(2,1)S(1)}, bf16[512,256]{1,0:T(8,128)(2,1)S(1)}, u32[]{:S(2)}, u32[]{:S(2)}) collective-permute-start(bf16[512,256]{1,0:T(8,128)(2,1)S(1)} %get-tuple-element.13), channel_id=1, source_target_pairs={{0,3},{1,0},{2,1},{3,2},{4,7},{5,4},{6,5},{7,6},{8,11},{9,8},{10,9... | collective-permute-start | bytes 786440 | tf_op jit(solution)/shard_map/ppermute | solution.py:442
  16.7 1.0 %copy-start = (bf16[2048,256]{1,0:T(8,128)(2,1)}, bf16[2048,256]{1,0:T(8,128)(2,1)S(1)}, u32[]{:S(2)}) copy-start(bf16[2048,256]{1,0:T(8,128)(2,1)S(1)} %constant_dynamic-update-slice_fusion.p_ref) | copy-start | bytes 3145732

commit v3 on v2

--- a/solution.py
+++ b/solution.py
@@ -441,7 +441,7 @@
     for m in range(1, C):
         got = lax.ppermute(projected, "col", [(c, (c + m) % C) for c in range(C)])
         inputs = lax.dynamic_update_slice(inputs, got, ((me + C - m) % C * n, 0))
-    S = 4
+    S = 2
     hb = n // S
     q = d // C
     bf16, f32 = jnp.bfloat16, jnp.float32
@@ -477,7 +477,7 @@
             dma((R - 1,)), dma((R - 1,)), dma((C - 1,)), dma((C - 1,)),
         ],
         compiler_params=pltpu.CompilerParams(
-            collective_id=0, has_side_effects=True, vmem_limit_bytes=58 * 2**20
+            collective_id=0, has_side_effects=True, vmem_limit_bytes=48 * 2**20
         ),
         cost_estimate=pl.CostEstimate(
             flops=4 * n * R * n * C * d, bytes_accessed=2 * n * R * n * C, transcendentals=n * d

time: 102 us -> 84.9 us (0.83)
  Pallas kernels: 85.3 us -> 73.4 us
  local copies, waits for them, and re-layouts: 7.37 us -> 2.84 us
    pallas_call x1, Pallas kernels: 77.4 us -> 65.3 us  [dense_body(): pl.pallas_call(functools.partial(layer_kernel, R, C, S, 1.0 / math.sqrt(n...]
    unnamed x6 -> x12, local copies, waits for them, and re-layouts: 7.22 us -> 2.7 us
  transfers between devices with their start and end apart: 3 -> 3, of which waited for: 1 -> 1; matrix products, arithmetic and copies ran while one was open for 0% -> 0% of each run, Pallas kernels for 8% -> 10%
where the time goes in v3:
time: 84.9 us; the launch traced here: 84.7 us
  Pallas kernels  73.4 us (86%)
  starting transfers between devices  4.46 us (5%)
  local copies, waits for them, and re-layouts  2.84 us (3%)
  between operations  1.43 us (2%)
  waiting for transfers between devices  1.39 us (2%)
  matrix products  1.22 us (1%)
    pallas_call x1, Pallas kernels, dense_body(): pl.pallas_call(functools.partial(layer_kernel, R, C, S, 1.0 / math.sqrt(n...  65.3 us
    pallas_call x1, Pallas kernels, build_dense(): pl.pallas_call(build_kernel, out_shape=jax.ShapeDtypeStruct((side * size,...  8.08 us
    ppermute x3, starting transfers between devices, dense_body(): got = lax.ppermute(projected, 'col', [(c, (c + m) % C) for c in range(C)])  4.46 us
    unnamed x12, local copies, waits for them, and re-layouts  2.7 us
  transfers between devices with their start and end apart: 3, of which 1 were waited for; matrix products, arithmetic and copies ran while one was open for 0% of the time, Pallas kernels for 10%

profile of v3, /device:TPU:0, one launch (start us, length us, event | category | flops | bytes accessed | tf_op | source)
XLA Modules:
  0.0 84.7 jit_solution(9266213060797007147)
XLA Ops:
  0.6 0.1 broadcast_in_dim.3
  0.7 1.2 %constant_dynamic-update-slice_fusion.3 = (bf16[2048,256]{1,0:T(8,128)(2,1)S(1)}, bf16[512,256]{1,0:T(8,128)(2,1)S(1)}) fusion(bf16[2048,256]{1,0:T(8,128)(2,1)S(1)} %broadcast_in_dim.3, s32[]{:T(128)S(6)} %select_n.27, bf16[512,256]{1,0:T(8,128)(2,1)} %feat_ref.1, bf16[256,256]{1,0:T(8,128)(2,1)} %w_ref.1), kind=kOutput, calls=%fused_computation.4 | convolution fusion | flops 67239936 | bytes 917508 | tf_op jit(solution)/shard_map/dot_general | solution.py:433
  1.9 0.5 collective-permute-start
  2.4 2.6 %collective-permute-start.1 = (bf16[512,256]{1,0:T(8,128)(2,1)S(1)}, bf16[512,256]{1,0:T(8,128)(2,1)S(1)}, u32[]{:S(2)}, u32[]{:S(2)}) collective-permute-start(bf16[512,256]{1,0:T(8,128)(2,1)S(1)} %get-tuple-element.13), channel_id=1, source_target_pairs={{0,2},{1,3},{2,0},{3,1},{4,6},{5,7},{6,4},{7,5},{8,10},{9,11},{10,... | collective-permute-start | bytes 786440 | tf_op jit(solution)/shard_map/ppermute | solution.py:442
  5.0 1.4 %collective-permute-start.2 = (bf16[512,256]{1,0:T(8,128)(2,1)S(1)}, bf16[512,256]{1,0:T(8,128)(2,1)S(1)}, u32[]{:S(2)}, u32[]{:S(2)}) collective-permute-start(bf16[512,256]{1,0:T(8,128)(2,1)S(1)} %get-tuple-element.13), channel_id=1, source_target_pairs={{0,3},{1,0},{2,1},{3,2},{4,7},{5,4},{6,5},{7,6},{8,11},{9,8},{10,9... | collective-permute-start | bytes 786440 | tf_op jit(solution)/shard_map/ppermute | solution.py:442
  7.1 0.0 copy-start
  7.1 0.0 copy-start.1
  7.1 0.0 copy-start.2
  7.1 0.0 copy-start.3
  7.1 8.1 %dense_cell.1.a_hbm = bf16[2048,2048]{1,0:T(8,128)(2,1)} custom-call(s32[1]{0:T(128)} %bitcast.8.count_ref, s32[256]{0:T(256)} %bitcast.12, s32[256]{0:T(256)} %bitcast.13, bf16[256,128,128]{2,1,0:T(8,128)(2,1)} %bitcast.11), custom_call_target="tpu_custom_call" | custom-call | flops 167772160 | bytes 16777216 | tf_op jit(solution)/shard_map/dense_cell/pallas_call | solution.py:163
  15.2 0.0 collective-permute-done
  15.2 0.0 collective-permute-done.1
  15.3 1.4 %collective-permute-done.2 = bf16[512,256]{1,0:T(8,128)(2,1)S(1)} collective-permute-done((bf16[512,256]{1,0:T(8,128)(2,1)S(1)}, bf16[512,256]{1,0:T(8,128)(2,1)S(1)}, u32[]{:S(2)}, u32[]{:S(2)}) %collective-permute-start.2) | collective-permute-done | bytes 262176 | tf_op jit(solution)/shard_map/ppermute | solution.py:442
  16.7 0.0 copy-done
  16.7 0.0 copy-done.1
  16.7 0.0 copy-done.2
  16.7 0.0 copy-done.3
  16.7 65.3 %layer.1 = (bf16[512,256]{1,0:T(8,128)(2,1)S(1)}, bf16[512,256]{1,0:T(8,128)(2,1)S(1)}, f32[256,256]{1,0:T(8,128)S(1)}, f32[1,256]{1,0:T(1,128)S(1)}) custom-call(bf16[2048,2048]{1,0:T(8,128)(2,1)} %dense_cell.1.a_hbm, bf16[2048,256]{1,0:T(8,128)(2,1)S(1)} %constant_dynamic-update-slice_fusion.p_ref, bf16[512,256]{1,0:T(8,128)(2,1)S(1)} %copy-done, ...), custom_call_target="tpu_custom_call" | custom-call | flops 4294967296 | bytes 8388608 | tf_op jit(solution)/shard_map/layer/pallas_call | solution.py:450
  82.1 0.7 copy.21
  82.8 0.7 copy.22
  83.5 0.7 copy.23
  84.2 0.6 copy.24
  (3 shorter events, 0.1 us)
Async XLA Ops:
  1.9 13.3 %collective-permute-start = (bf16[512,256]{1,0:T(8,128)(2,1)S(1)}, bf16[512,256]{1,0:T(8,128)(2,1)S(1)}, u32[]{:S(2)}, u32[]{:S(2)}) collective-permute-start(bf16[512,256]{1,0:T(8,128)(2,1)S(1)} %get-tuple-element.13), channel_id=1, source_target_pairs={{0,1},{1,2},{2,3},{3,0},{4,5},{5,6},{6,7},{7,4},{8,9},{9,10},{10,1... | collective-permute-start | bytes 786440 | tf_op jit(solution)/shard_map/ppermute | solution.py:442
  2.4 12.8 %collective-permute-start.1 = (bf16[512,256]{1,0:T(8,128)(2,1)S(1)}, bf16[512,256]{1,0:T(8,128)(2,1)S(1)}, u32[]{:S(2)}, u32[]{:S(2)}) collective-permute-start(bf16[512,256]{1,0:T(8,128)(2,1)S(1)} %get-tuple-element.13), channel_id=1, source_target_pairs={{0,2},{1,3},{2,0},{3,1},{4,6},{5,7},{6,4},{7,5},{8,10},{9,11},{10,... | collective-permute-start | bytes 786440 | tf_op jit(solution)/shard_map/ppermute | solution.py:442
  5.0 11.7 %collective-permute-start.2 = (bf16[512,256]{1,0:T(8,128)(2,1)S(1)}, bf16[512,256]{1,0:T(8,128)(2,1)S(1)}, u32[]{:S(2)}, u32[]{:S(2)}) collective-permute-start(bf16[512,256]{1,0:T(8,128)(2,1)S(1)} %get-tuple-element.13), channel_id=1, source_target_pairs={{0,3},{1,0},{2,1},{3,2},{4,7},{5,4},{6,5},{7,6},{8,11},{9,8},{10,9... | collective-permute-start | bytes 786440 | tf_op jit(solution)/shard_map/ppermute | solution.py:442
  7.1 9.6 %copy-start = (bf16[512,256]{1,0:T(8,128)(2,1)S(1)}, bf16[512,256]{1,0:T(8,128)(2,1)}, u32[]{:S(2)}) copy-start(bf16[512,256]{1,0:T(8,128)(2,1)} %feat_ref.1) | copy-start | bytes 786436
  7.1 9.6 %copy-start.1 = (bf16[256,256]{1,0:T(8,128)(2,1)S(1)}, bf16[256,256]{1,0:T(8,128)(2,1)}, u32[]{:S(2)}) copy-start(bf16[256,256]{1,0:T(8,128)(2,1)} %w_ref.1) | copy-start | bytes 393220
  7.1 9.6 %copy-start.2 = (bf16[512,256]{1,0:T(8,128)(2,1)S(1)}, bf16[512,256]{1,0:T(8,128)(2,1)}, u32[]{:S(2)}) copy-start(bf16[512,256]{1,0:T(8,128)(2,1)} %cot_ref.1) | copy-start | bytes 786436
  7.1 9.6 %copy-start.3 = (f32[256]{0:T(256)S(1)}, f32[256]{0:T(256)}, u32[]{:S(2)}) copy-start(f32[256]{0:T(256)} %param.10) | copy-start | bytes 3076
